TPU v7x, 128 devices: a whole 4x4x4 slice. The times are simulated.
128 devices in a mesh: feat: 8 (over x, core), rows: 16 (over z, y).
Axes of the slice: x: 4, y: 4, z: 4, core: 2. Of those that a mesh axis runs over, the one named last changes fastest.
Arguments:
- features: bfloat16 [128, 128, 768], P('feat', None, 'rows'), may hold values from -6 to 6
- w_in: bfloat16 [128, 256], replicated, may hold values from -0.5 to 0.5
- bias: float32 [256], replicated, may hold values from -4 to 4
- tiles: bfloat16 [768, 8, 128, 128], P(('feat', 'rows')), may hold values from 0 to 1, as said below
- tile_cols: int32 [768, 8], P(('feat', 'rows')), may hold values from 0 to 767, as said below
- tile_counts: int32 [768], P(('feat', 'rows')), may hold values from 1 to 8, as said below
- cotangent: bfloat16 [98304, 256], P(('feat', 'rows')), may hold values from -6 to 6
Outputs:
- hidden: bfloat16 [98304, 256], P(('feat', 'rows'))
- weight_grad: float32 [128, 256], P('feat')
Inputs may be any that keep to these rules, and one draw needn't show every extreme that they name: Each block row's count lies between 1 and 8; in every draw some device owns a block row with 8 live slots. Slots k >= tile_counts[I] are ignored. `tile_cols`: block row I on the device owning blocks s * 6 to s * 6 + 6 - 1 (s = I // 6) names column blocks J with J // 96 = I // 96 and (J - (s % 16) * 6 + 2) mod 96 below 10: its own blocks or up to 2 blocks of the neighbouring devices in its cycle, wrapping; both ends are reached. `tiles`: entries are 0 or 1.
All inputs are finite; a program needn't handle non-finite values.
Results may differ from a plain program's by a relative error of at most 0.008.
Values may be sent and summed in bfloat16 or wider, within the bound.
No kernel may reach another device: no remote copies, remote signals or barrier semaphores. Data moves between devices by JAX's collectives and lax.ppermute only.
A program may use at most 64 MiB of HBM per device.

v0:
```python
import jax
import jax.numpy as jnp
from jax import lax
from jax.sharding import PartitionSpec as P

HALO_BLK = 2


def padded(cells, sides, width):
    for axis, dim in sides:
        count = lax.axis_size(axis)
        head = lax.slice_in_dim(cells, 0, width, axis=dim)
        tail = lax.slice_in_dim(cells, cells.shape[dim] - width, cells.shape[dim], axis=dim)
        cells = jnp.concatenate(
            [
                lax.ppermute(tail, axis, [(i, (i + 1) % count) for i in range(count)]),
                cells,
                lax.ppermute(head, axis, [((i + 1) % count, i) for i in range(count)]),
            ],
            axis=dim,
        )
    return cells


def shifted(block, axis, distance):
    devices = range(lax.axis_size(axis))
    route = [((i - distance) % len(devices), i) for i in devices]
    return lax.ppermute(block, axis, route)


def gelu_parts(values):
    inner = 0.7978845608 * (values + 0.044715 * values * values * values)
    tangent = jnp.tanh(inner)
    output = 0.5 * values * (1.0 + tangent)
    slope = 0.5 * (1.0 + tangent) + 0.5 * values * (1.0 - tangent * tangent) * 0.7978845608 * (
        1.0 + 3.0 * 0.044715 * values * values
    )
    return (output, slope)


def halo_projected(projected, margin):
    return padded(projected, (("rows", 0),), margin)


def body(features, w_in, bias, tiles, tile_cols, tile_counts, cotangent):
    block_rows, slot_count, tile_side, unused_side = tiles.shape
    hidden_width = w_in.shape[1]
    feat_size = lax.axis_size("feat")
    row_size = lax.axis_size("rows")
    slice_width = w_in.shape[0] // feat_size
    nodes_dev = block_rows * tile_side
    sub_rows = nodes_dev // row_size
    feat_id = lax.axis_index("feat")
    row_id = lax.axis_index("rows")
    margin = HALO_BLK * tile_side
    w_own = lax.dynamic_slice_in_dim(w_in, feat_id * slice_width, slice_width, 0)
    partial_value = jnp.einsum(
        "cdn,ch->dnh", features, w_own, preferred_element_type=jnp.float32
    ).astype(jnp.bfloat16)
    received = lax.all_to_all(
        partial_value, ("feat", "rows"), split_axis=0, concat_axis=0, tiled=True
    )
    received = received.reshape(feat_size, nodes_dev, hidden_width)
    projected = jnp.sum(received.astype(jnp.float32), axis=0).astype(jnp.bfloat16)
    extended = halo_projected(projected, margin)
    ext_count = block_rows + 2 * HALO_BLK
    ext_blocks = extended.reshape(ext_count, tile_side, hidden_width)
    cycle_size = block_rows * row_size
    local_cols = (tile_cols - feat_id * cycle_size - row_id * block_rows + HALO_BLK) % cycle_size
    slot_ids = jnp.arange(slot_count, dtype=jnp.int32)
    live_slot = (slot_ids[None, :] < tile_counts[:, None]).astype(jnp.bfloat16)
    masked = tiles * live_slot[:, :, None, None]
    degree = jnp.sum(masked, axis=(1, 3), dtype=jnp.float32)
    neighbours = ext_blocks[local_cols]
    summed_rows = jnp.einsum(
        "bkij,bkjh->bih", masked, neighbours, preferred_element_type=jnp.float32
    )
    own_rows = projected.reshape(block_rows, tile_side, hidden_width).astype(jnp.float32)
    pre_act = (own_rows + summed_rows) / (degree[:, :, None] + 1.0) + bias
    activated, slope = gelu_parts(pre_act)
    hidden = activated.astype(jnp.bfloat16).reshape(nodes_dev, hidden_width)
    scaled = (
        cotangent.reshape(block_rows, tile_side, hidden_width).astype(jnp.float32)
        * slope
        / (degree[:, :, None] + 1.0)
    ).astype(jnp.bfloat16)
    targets = jnp.arange(ext_count, dtype=jnp.int32)
    onehot = (local_cols[:, :, None] == targets[None, None, :]).astype(jnp.bfloat16)
    combined = jnp.einsum(
        "bkq,bkij->qbij", onehot, masked, preferred_element_type=jnp.float32
    ).astype(jnp.bfloat16)
    ext_sums = jnp.einsum("qbij,bih->qjh", combined, scaled, preferred_element_type=jnp.float32)
    from_before = shifted(ext_sums[block_rows + HALO_BLK :].astype(jnp.bfloat16), "rows", 1).astype(
        jnp.float32
    )
    from_after = shifted(ext_sums[:HALO_BLK].astype(jnp.bfloat16), "rows", -1).astype(jnp.float32)
    own_sums = ext_sums[HALO_BLK : HALO_BLK + block_rows] + scaled.astype(jnp.float32)
    own_sums = own_sums.at[:HALO_BLK].add(from_before)
    own_sums = own_sums.at[block_rows - HALO_BLK :].add(from_after)
    grad_proj = own_sums.astype(jnp.bfloat16).reshape(nodes_dev, hidden_width)
    pieces = lax.all_to_all(
        grad_proj.reshape(row_size, sub_rows, hidden_width),
        "rows",
        split_axis=0,
        concat_axis=0,
        tiled=True,
    )
    grad_slice = jnp.einsum(
        "cdn,dnh->ch",
        features,
        lax.all_gather(pieces, "feat", axis=0, tiled=True),
        preferred_element_type=jnp.float32,
    )
    weight_grad = lax.psum(grad_slice, "rows")
    return (hidden, weight_grad)


def solution(mesh):
    in_specs = (
        P("feat", None, "rows"),
        P(),
        P(),
        P(("feat", "rows"), None, None, None),
        P(("feat", "rows"), None),
        P(("feat", "rows")),
        P(("feat", "rows"), None),
    )
    out_specs = (P(("feat", "rows"), None), P("feat", None))
    return jax.shard_map(body, mesh=mesh, in_specs=in_specs, out_specs=out_specs, check_vma=False)
```

profile of v0, /device:TPU:0, one launch (start us, length us, event | category | flops | bytes accessed | tf_op | source)
XLA Modules:
  0.0 216.6 jit_solution(2524314712389904341)
XLA Ops:
  7.2 0.0 copy-start
  7.2 0.8 copy-done
  8.0 1.9 convert_bitcast_fusion.1
  9.9 3.2 %copy.17 = bf16[128,48,256]{2,1,0:T(8,128)(2,1)} copy(bf16[128,48,256]{0,2,1:T(8,128)(2,1)S(1)} %convert_bitcast_fusion.1) | data formatting | bytes 6291456 | tf_op jit(solution)/shard_map/convert_element_type | solution.py:59
  13.1 0.0 copy-start.9
  13.1 0.0 copy-start.8
  13.1 11.1 %all-to-all-start = ((bf16[128,48,256]{2,1,0:T(8,128)(2,1)}), bf16[128,48,256]{2,1,0:T(8,128)(2,1)S(1)}, u32[]{:S(2)}, u32[]{:S(2)}) async-start(bf16[128,48,256]{2,1,0:T(8,128)(2,1)} %copy.17), calls=%async_computation | async-start | bytes 6291456 | tf_op jit(solution)/shard_map/all_to_all | solution.py:60
  24.3 0.0 all-gather.2.cloned.1.call-start
  24.3 0.0 copy-done.9
  24.3 0.1 fusion.27
  24.4 0.0 copy-done.8
  24.4 2.0 convert_reduce_fusion
  26.5 0.0 copy-start.1
  26.5 1.1 copy-done.1
  27.6 3.1 %convert_bitcast_fusion = bf16[10,6,128,128]{3,0,2,1:T(8,128)(2,1)} fusion(bf16[6,8,128,128]{3,2,1,0:T(8,128)(2,1)S(1)} %get-tuple-element.27, s32[6,8]{1,0:T(8,128)S(1)} %get-tuple-element.29), kind=kOutput, calls=%fused_computation.2 | convolution fusion | flops 16712160 | bytes 3539136 | tf_op jit(solution)/shard_map/bkq,bkij->qbij/dot_general | solution.py:89
  30.7 33.8 %all-to-all-done = bf16[128,48,256]{2,1,0:T(8,128)(2,1)S(1)} async-done(((bf16[128,48,256]{2,1,0:T(8,128)(2,1)}), bf16[128,48,256]{2,1,0:T(8,128)(2,1)S(1)}, u32[]{:S(2)}, u32[]{:S(2)}) %all-to-all-start) | async-done | bytes 3145760 | tf_op jit(solution)/shard_map/all_to_all | solution.py:60
  64.5 0.4 bitcast_reduce_fusion
  64.9 0.0 copy-start.4
  65.0 0.7 copy-done.4
  65.7 0.7 collective-permute-start
  66.4 4.7 %collective-permute-start.1 = (bf16[256,256]{1,0:T(8,128)(2,1)S(1)}, bf16[256,256]{1,0:T(8,128)(2,1)S(1)}, u32[]{:S(2)}, u32[]{:S(2)}) collective-permute-start(bf16[256,256]{1,0:T(8,128)(2,1)S(1)} %get-tuple-element.35), channel_id=1, source_target_pairs={{1,0},{2,1},{3,2},{4,3},{5,4},{6,5},{7,6},{8,7},{9,8},{10,9},{11,1... | collective-permute-start | bytes 393224 | tf_op jit(solution)/shard_map/ppermute | solution.py:18
  71.1 0.1 reshape.114
  71.2 2.9 %collective-permute-done = bf16[256,256]{1,0:T(8,128)(2,1)S(1)} collective-permute-done((bf16[256,256]{1,0:T(8,128)(2,1)S(1)}, bf16[256,256]{1,0:T(8,128)(2,1)S(1)}, u32[]{:S(2)}, u32[]{:S(2)}) %collective-permute-start) | collective-permute-done | bytes 131104 | tf_op jit(solution)/shard_map/ppermute | solution.py:16
  74.1 0.0 collective-permute-done.1
  74.1 1.0 pad_maximum_fusion
  75.1 0.0 copy-start.2
  75.1 0.0 copy-start.5
  75.1 0.0 copy-start.10
  75.2 2.5 %gather_fusion = bf16[48,128,256]{2,1,0:T(8,128)(2,1)} fusion(bf16[10,128,256]{2,1,0:T(8,128)(2,1)S(1)} %bitcast.47, s32[1024]{0:T(1024)S(1)} %pad_clamp_fusion), kind=kCustom, calls=%fused_computation | custom fusion | bytes 6291648 | tf_op jit(solution)/shard_map/gather | solution.py:74
  77.7 0.0 copy-done.2
  77.7 0.0 copy-done.5
  77.7 0.0 copy-done.10
  77.7 0.0 copy-start.3
  77.7 0.0 copy-start.7
  77.7 2.8 %fusion.8 = f32[6,128,256]{2,1,0:T(8,128)S(1)} fusion(bf16[6,8,128,128]{3,2,1,0:T(8,128)(2,1)S(1)} %copy-done.2, bf16[6,8,128,256]{3,2,1,0:T(8,128)(2,1)} %bitcast.49, bf16[6,128,256]{2,1,0:T(8,128)(2,1)S(1)} %bitcast.50, f32[256]{0:T(256)S(1)} %copy-done.10, f32[6,128]{1,0:T(8,128)S(1)} %broadcast_add_fusion), kind=kOutput, calls=%fused_computation.12 | convolution fusion | flops 403439616 | bytes 5902336 | tf_op jit(solution)/shard_map/bkij,bkjh->bih/dot_general | solution.py:75
  80.5 0.0 copy-done.3
  80.5 0.1 copy-done.7
  80.6 1.5 fusion.32
  82.1 0.1 collective-permute-start.2
  82.2 0.0 copy-start.6
  82.2 1.4 slice_add_fusion
  83.6 5.3 %collective-permute-start.3 = (bf16[2,128,256]{2,1,0:T(8,128)(2,1)S(1)}, bf16[2,128,256]{2,1,0:T(8,128)(2,1)S(1)}, u32[]{:S(2)}, u32[]{:S(2)}) collective-permute-start(bf16[2,128,256]{2,1,0:T(8,128)(2,1)S(1)} %get-tuple-element.32), channel_id=1, source_target_pairs={{1,0},{2,1},{3,2},{4,3},{5,4},{6,5},{7,6},{8,7},{9,8},{10,9},{11,1... | collective-permute-start | bytes 393224 | tf_op jit(solution)/shard_map/ppermute | solution.py:28
  88.9 1.6 collective-permute-done.2
  90.5 0.1 fusion.19
  90.5 0.9 collective-permute-done.3
  91.4 0.1 fusion.18
  91.5 16.3 %all_to_all.10 = bf16[16,48,256]{2,1,0:T(8,128)(2,1)S(1)} all-to-all(bf16[16,48,256]{2,1,0:T(8,128)(2,1)S(1)} %bitcast.51), channel_id=1, replica_groups=mesh['feat'=8,'rows'=16] {'rows'}, dimensions={0} | all-to-all | bytes 786432 | tf_op jit(solution)/shard_map/all_to_all | solution.py:101
  107.9 0.9 copy.20
  108.8 0.0 all-gather.2.cloned.1.call-update
  108.8 24.0 %all-gather.2.cloned.1.call-done = bf16[128,48,256]{2,0,1:T(8,128)(2,1)} async-done(((bf16[16,48,256]{2,0,1:T(8,128)(2,1)}), bf16[128,48,256]{2,0,1:T(8,128)(2,1)}) %all-gather.2.cloned.1.call-update) | async-done | bytes 3145744 | tf_op jit(solution)/shard_map/all_gather | solution.py:111
  132.8 0.0 copy-done.6
  132.8 2.4 %convolution_bitcast_fusion.1 = f32[16,256]{1,0:T(8,128)S(1)} fusion(bf16[128,48,256]{2,0,1:T(8,128)(2,1)} %all-gather.2.cloned.1.call-done, bf16[16,128,48]{1,2,0:T(8,128)(2,1)S(1)} %copy-done.6), kind=kOutput, calls=%fused_computation.15 | convolution fusion | flops 50331648 | bytes 3358720 | tf_op jit(solution)/shard_map/cdn,dnh->ch/dot_general | solution.py:108
  135.2 74.5 %psum.7 = f32[16,256]{1,0:T(8,128)} all-reduce(f32[16,256]{1,0:T(8,128)S(1)} %convolution_bitcast_fusion.1), channel_id=1, replica_groups=mesh['feat'=8,'rows'=16] {'rows'}, use_global_device_ids=true, to_apply=%region_2.3 | all-reduce | flops 4096 | bytes 32768 | tf_op jit(solution)/shard_map/psum | solution.py:114
  (6 shorter events, 0.1 us)
Async XLA Ops:
  7.2 0.8 copy-start
  13.1 11.2 %copy-start.9 = (s32[6]{0:T(128)S(1)}, s32[6]{0:T(128)}, u32[]{:S(2)}) copy-start(s32[6]{0:T(128)} %param.16) | copy-start | bytes 76
  13.1 11.3 %copy-start.8 = (s32[6,8]{1,0:T(8,128)S(1)}, s32[6,8]{1,0:T(8,128)}, u32[]{:S(2)}) copy-start(s32[6,8]{1,0:T(8,128)} %param.15) | copy-start | bytes 580
  13.1 51.4 %all-to-all-start = ((bf16[128,48,256]{2,1,0:T(8,128)(2,1)}), bf16[128,48,256]{2,1,0:T(8,128)(2,1)S(1)}, u32[]{:S(2)}, u32[]{:S(2)}) async-start(bf16[128,48,256]{2,1,0:T(8,128)(2,1)} %copy.17), calls=%async_computation | async-start | bytes 6291456 | tf_op jit(solution)/shard_map/all_to_all | solution.py:60
  24.3 108.5 %all-gather.2.cloned.1.call-start = ((), (), s32[]{:S(2)}) async-start(), calls=%async_computation.2 | async-start | bytes 3538944 | tf_op jit(solution)/shard_map/all_gather | solution.py:111
  26.5 1.1 copy-start.1
  64.9 0.7 copy-start.4
  65.7 8.4 %collective-permute-start = (bf16[256,256]{1,0:T(8,128)(2,1)S(1)}, bf16[256,256]{1,0:T(8,128)(2,1)S(1)}, u32[]{:S(2)}, u32[]{:S(2)}) collective-permute-start(bf16[256,256]{1,0:T(8,128)(2,1)S(1)} %get-tuple-element.34), channel_id=1, source_target_pairs={{0,1},{1,2},{2,3},{3,4},{4,5},{5,6},{6,7},{7,8},{8,9},{9,10},{10,1... | collective-permute-start | bytes 393224 | tf_op jit(solution)/shard_map/ppermute | solution.py:16
  66.4 7.7 %collective-permute-start.1 = (bf16[256,256]{1,0:T(8,128)(2,1)S(1)}, bf16[256,256]{1,0:T(8,128)(2,1)S(1)}, u32[]{:S(2)}, u32[]{:S(2)}) collective-permute-start(bf16[256,256]{1,0:T(8,128)(2,1)S(1)} %get-tuple-element.35), channel_id=1, source_target_pairs={{1,0},{2,1},{3,2},{4,3},{5,4},{6,5},{7,6},{8,7},{9,8},{10,9},{11,1... | collective-permute-start | bytes 393224 | tf_op jit(solution)/shard_map/ppermute | solution.py:18
  75.1 2.6 %copy-start.2 = (bf16[6,8,128,128]{3,2,1,0:T(8,128)(2,1)S(1)}, bf16[6,8,128,128]{3,2,1,0:T(8,128)(2,1)}, u32[]{:S(2)}) copy-start(bf16[6,8,128,128]{3,2,1,0:T(8,128)(2,1)} %copy-done.1) | copy-start | bytes 4718596
  75.1 2.6 %copy-start.5 = (bf16[768,256]{1,0:T(8,128)(2,1)S(1)}, bf16[768,256]{1,0:T(8,128)(2,1)}, u32[]{:S(2)}) copy-start(bf16[768,256]{1,0:T(8,128)(2,1)} %copy-done.4) | copy-start | bytes 1179652
  75.1 2.6 %copy-start.10 = (f32[256]{0:T(256)S(1)}, f32[256]{0:T(256)}, u32[]{:S(2)}) copy-start(f32[256]{0:T(256)} %param.13) | copy-start | bytes 3076
  77.7 2.8 %copy-start.3 = (bf16[10,6,128,128]{3,0,2,1:T(8,128)(2,1)S(1)}, bf16[10,6,128,128]{3,0,2,1:T(8,128)(2,1)}, u32[]{:S(2)}) copy-start(bf16[10,6,128,128]{3,0,2,1:T(8,128)(2,1)} %convert_bitcast_fusion) | copy-start | bytes 5898244
  77.7 2.9 %copy-start.7 = (bf16[768,256]{1,0:T(8,128)(2,1)S(1)}, bf16[768,256]{1,0:T(8,128)(2,1)}, u32[]{:S(2)}) copy-start(bf16[768,256]{1,0:T(8,128)(2,1)} %param.17) | copy-start | bytes 1179652
  82.1 8.4 %collective-permute-start.2 = (bf16[2,128,256]{2,1,0:T(8,128)(2,1)S(1)}, bf16[2,128,256]{2,1,0:T(8,128)(2,1)S(1)}, u32[]{:S(2)}, u32[]{:S(2)}) collective-permute-start(bf16[2,128,256]{2,1,0:T(8,128)(2,1)S(1)} %get-tuple-element.33), channel_id=1, source_target_pairs={{15,0},{0,1},{1,2},{2,3},{3,4},{4,5},{5,6},{6,7},{7,8},{8,9},{9,10... | collective-permute-start | bytes 393224 | tf_op jit(solution)/shard_map/ppermute | solution.py:28
  82.2 50.6 %copy-start.6 = (bf16[16,128,48]{1,2,0:T(8,128)(2,1)S(1)}, bf16[16,128,48]{1,2,0:T(8,128)(2,1)}, u32[]{:S(2)}) copy-start(bf16[16,128,48]{1,2,0:T(8,128)(2,1)} %param.11) | copy-start | bytes 589828
  83.6 7.9 %collective-permute-start.3 = (bf16[2,128,256]{2,1,0:T(8,128)(2,1)S(1)}, bf16[2,128,256]{2,1,0:T(8,128)(2,1)S(1)}, u32[]{:S(2)}, u32[]{:S(2)}) collective-permute-start(bf16[2,128,256]{2,1,0:T(8,128)(2,1)S(1)} %get-tuple-element.32), channel_id=1, source_target_pairs={{1,0},{2,1},{3,2},{4,3},{5,4},{6,5},{7,6},{8,7},{9,8},{10,9},{11,1... | collective-permute-start | bytes 393224 | tf_op jit(solution)/shard_map/ppermute | solution.py:28
Sparse Core Ops, SparseCore 0:
  108.9 23.8 all-gather.1
where the time goes:
time: 217 us
  blocking collectives  90.9 us (42%)
  waiting for transfers between devices  63.2 us (29%)
  starting transfers between devices  22 us (10%)
  between operations  14.2 us (7%)
  matrix products  11.6 us (5%)
  local copies, waits for them, and re-layouts  9.55 us (4%)
  other arithmetic  5.11 us (2%)
    psum x1, blocking collectives, body(): weight_grad = lax.psum(grad_slice, 'rows')  74.5 us
    all_to_all x1, waiting for transfers between devices, body(): lax.all_to_all(partial_value, ('feat', 'rows'), split_axis=0, concat_axis...  33.8 us
    all_gather x1, waiting for transfers between devices, body(): lax.all_gather(pieces, 'feat', axis=0, tiled=True)  24 us
    all_to_all x1, blocking collectives, body(): lax.all_to_all(grad_proj.reshape(row_size, sub_rows, hidden_width), 'rows...  16.3 us
    all_to_all x1, starting transfers between devices, body(): lax.all_to_all(partial_value, ('feat', 'rows'), split_axis=0, concat_axis...  11.1 us
    ppermute x2, starting transfers between devices, shifted(): return lax.ppermute(block, axis, route)  5.42 us
    ppermute x1, starting transfers between devices, padded(): lax.ppermute(head, axis, [((i + 1) % count, i) for i in range(count)])  4.74 us
  transfers between devices with their start and end apart: 6, of which 5 were waited for; matrix products, arithmetic and copies ran while one was open for 3% of the time, Pallas kernels for 0%

commit v1 on v0

--- a/solution.py
+++ b/solution.py
@@ -105,12 +105,27 @@
         concat_axis=0,
         tiled=True,
     )
-    grad_slice = jnp.einsum(
+    size, here = (lax.axis_size("feat"), lax.axis_index("feat"))
+    left = [(i_2, (i_2 - 1) % size) for i_2 in range(size)]
+    extent = pieces.shape[0]
+    held = pieces
+    so_far = jnp.einsum(
         "cdn,dnh->ch",
-        features,
-        lax.all_gather(pieces, "feat", axis=0, tiled=True),
+        lax.dynamic_slice_in_dim(features, here * extent, held.shape[0], axis=1),
+        held,
         preferred_element_type=jnp.float32,
     )
+    for turn in range(1, size):
+        held = lax.ppermute(held, "feat", left)
+        so_far = so_far + jnp.einsum(
+            "cdn,dnh->ch",
+            lax.dynamic_slice_in_dim(
+                features, (here + turn) % size * extent, held.shape[0], axis=1
+            ),
+            held,
+            preferred_element_type=jnp.float32,
+        )
+    grad_slice = so_far
     weight_grad = lax.psum(grad_slice, "rows")
     return (hidden, weight_grad)
 

time: 217 us -> 228 us (1.051)
  starting transfers between devices: 22 us -> 40.7 us
  between operations: 14.2 us -> 0.92 us
  waiting for transfers between devices: 63.2 us -> 71.7 us
  blocking collectives: 90.9 us -> 86.9 us
    ppermute x0 -> x7, waiting for transfers between devices: none -> 32.4 us  [body(): held = lax.ppermute(held, 'feat', left)]
    all_gather x1 -> x0, waiting for transfers between devices: 24 us -> none  [body(): lax.all_gather(pieces, 'feat', axis=0, tiled=True)]
    ppermute x0 -> x7, starting transfers between devices: none -> 18.7 us  [body(): held = lax.ppermute(held, 'feat', left)]
    psum x1, blocking collectives: 74.5 us -> 70.6 us  [body(): weight_grad = lax.psum(grad_slice, 'rows')]
    unnamed x22 -> x34, local copies, waits for them, and re-layouts: 2.84 us -> 4.56 us
  transfers between devices with their start and end apart: 6 -> 12, of which waited for: 5 -> 11; matrix products, arithmetic and copies ran while one was open for 3% -> 5% of each run, Pallas kernels for 0% -> 0%
where the time goes in v1:
time: 228 us
  blocking collectives  86.9 us (38%)
  waiting for transfers between devices  71.7 us (31%)
  starting transfers between devices  40.7 us (18%)
  matrix products  11.7 us (5%)
  local copies, waits for them, and re-layouts  10.9 us (5%)
  other arithmetic  5.11 us (2%)
    psum x1, blocking collectives, body(): weight_grad = lax.psum(grad_slice, 'rows')  70.6 us
    all_to_all x1, waiting for transfers between devices, body(): lax.all_to_all(partial_value, ('feat', 'rows'), split_axis=0, concat_axis...  33.9 us
    ppermute x7, waiting for transfers between devices, body(): held = lax.ppermute(held, 'feat', left)  32.4 us
    ppermute x7, starting transfers between devices, body(): held = lax.ppermute(held, 'feat', left)  18.7 us
    all_to_all x1, blocking collectives, body(): lax.all_to_all(grad_proj.reshape(row_size, sub_rows, hidden_width), 'rows...  16.3 us
    all_to_all x1, starting transfers between devices, body(): lax.all_to_all(partial_value, ('feat', 'rows'), split_axis=0, concat_axis...  11.1 us
    ppermute x2, starting transfers between devices, shifted(): return lax.ppermute(block, axis, route)  5.42 us
    ppermute x1, starting transfers between devices, padded(): lax.ppermute(head, axis, [((i + 1) % count, i) for i in range(count)])  4.74 us
  transfers between devices with their start and end apart: 12, of which 11 were waited for; matrix products, arithmetic and copies ran while one was open for 5% of the time, Pallas kernels for 0%

profile of v1, /device:TPU:0, one launch (start us, length us, event | category | flops | bytes accessed | tf_op | source)
XLA Modules:
  0.0 227.9 jit_solution(1332541207921715408)
XLA Ops:
  0.6 0.0 copy-start
  0.7 0.8 copy-done
  1.5 1.9 convert_bitcast_fusion.1
  3.4 3.2 %copy.29 = bf16[128,48,256]{2,1,0:T(8,128)(2,1)} copy(bf16[128,48,256]{0,2,1:T(8,128)(2,1)S(1)} %convert_bitcast_fusion.1) | data formatting | bytes 6291456 | tf_op jit(solution)/shard_map/convert_element_type | solution.py:59
  6.6 11.1 %all-to-all-start = ((bf16[128,48,256]{2,1,0:T(8,128)(2,1)}), bf16[128,48,256]{2,1,0:T(8,128)(2,1)S(1)}, u32[]{:S(2)}, u32[]{:S(2)}) async-start(bf16[128,48,256]{2,1,0:T(8,128)(2,1)} %copy.29), calls=%async_computation | async-start | bytes 6291456 | tf_op jit(solution)/shard_map/all_to_all | solution.py:60
  17.8 0.1 fusion.33
  17.9 2.0 convert_reduce_fusion
  19.9 1.1 copy-done.2
  21.1 3.1 %convert_bitcast_fusion = bf16[10,6,128,128]{3,0,2,1:T(8,128)(2,1)} fusion(bf16[6,8,128,128]{3,2,1,0:T(8,128)(2,1)S(1)} %get-tuple-element.27, s32[6,8]{1,0:T(8,128)S(1)} %get-tuple-element.29), kind=kOutput, calls=%fused_computation.2 | convolution fusion | flops 16712160 | bytes 3539136 | tf_op jit(solution)/shard_map/bkq,bkij->qbij/dot_general | solution.py:89
  24.1 33.9 %all-to-all-done = bf16[128,48,256]{2,1,0:T(8,128)(2,1)S(1)} async-done(((bf16[128,48,256]{2,1,0:T(8,128)(2,1)}), bf16[128,48,256]{2,1,0:T(8,128)(2,1)S(1)}, u32[]{:S(2)}, u32[]{:S(2)}) %all-to-all-start) | async-done | bytes 3145760 | tf_op jit(solution)/shard_map/all_to_all | solution.py:60
  58.0 0.4 bitcast_reduce_fusion
  58.4 0.0 copy-start.5
  58.5 0.7 copy-done.5
  59.2 0.7 collective-permute-start
  59.9 4.7 %collective-permute-start.1 = (bf16[256,256]{1,0:T(8,128)(2,1)S(1)}, bf16[256,256]{1,0:T(8,128)(2,1)S(1)}, u32[]{:S(2)}, u32[]{:S(2)}) collective-permute-start(bf16[256,256]{1,0:T(8,128)(2,1)S(1)} %get-tuple-element.35), channel_id=1, source_target_pairs={{1,0},{2,1},{3,2},{4,3},{5,4},{6,5},{7,6},{8,7},{9,8},{10,9},{11,1... | collective-permute-start | bytes 393224 | tf_op jit(solution)/shard_map/ppermute | solution.py:18
  64.6 0.1 reshape.114
  64.7 2.9 %collective-permute-done = bf16[256,256]{1,0:T(8,128)(2,1)S(1)} collective-permute-done((bf16[256,256]{1,0:T(8,128)(2,1)S(1)}, bf16[256,256]{1,0:T(8,128)(2,1)S(1)}, u32[]{:S(2)}, u32[]{:S(2)}) %collective-permute-start) | collective-permute-done | bytes 131104 | tf_op jit(solution)/shard_map/ppermute | solution.py:16
  67.6 1.0 pad_maximum_fusion
  68.6 2.5 %gather_fusion = bf16[48,128,256]{2,1,0:T(8,128)(2,1)} fusion(bf16[10,128,256]{2,1,0:T(8,128)(2,1)S(1)} %bitcast.88, s32[1024]{0:T(1024)S(1)} %pad_clamp_fusion), kind=kCustom, calls=%fused_computation | custom fusion | bytes 6291648 | tf_op jit(solution)/shard_map/gather | solution.py:74
  71.2 0.0 copy-start.7
  71.2 2.8 %fusion.8 = f32[6,128,256]{2,1,0:T(8,128)S(1)} fusion(bf16[6,8,128,128]{3,2,1,0:T(8,128)(2,1)S(1)} %copy-done.3, bf16[6,8,128,256]{3,2,1,0:T(8,128)(2,1)} %bitcast.90, bf16[6,128,256]{2,1,0:T(8,128)(2,1)S(1)} %bitcast.91, f32[256]{0:T(256)S(1)} %copy-done.12, f32[6,128]{1,0:T(8,128)S(1)} %broadcast_add_fusion), kind=kOutput, calls=%fused_computation.12 | convolution fusion | flops 403439616 | bytes 5902336 | tf_op jit(solution)/shard_map/bkij,bkjh->bih/dot_general | solution.py:75
  74.0 0.0 copy-done.4
  74.0 0.1 copy-done.7
  74.1 1.5 fusion.38
  75.6 0.1 collective-permute-start.2
  75.7 1.4 slice_add_fusion
  77.1 5.3 %collective-permute-start.3 = (bf16[2,128,256]{2,1,0:T(8,128)(2,1)S(1)}, bf16[2,128,256]{2,1,0:T(8,128)(2,1)S(1)}, u32[]{:S(2)}, u32[]{:S(2)}) collective-permute-start(bf16[2,128,256]{2,1,0:T(8,128)(2,1)S(1)} %get-tuple-element.32), channel_id=1, source_target_pairs={{1,0},{2,1},{3,2},{4,3},{5,4},{6,5},{7,6},{8,7},{9,8},{10,9},{11,1... | collective-permute-start | bytes 393224 | tf_op jit(solution)/shard_map/ppermute | solution.py:28
  82.4 1.6 collective-permute-done.2
  84.0 0.1 fusion.26
  84.0 0.9 collective-permute-done.3
  84.9 0.1 fusion.25
  85.0 16.3 %all_to_all.10 = bf16[16,48,256]{2,1,0:T(8,128)(2,1)S(1)} all-to-all(bf16[16,48,256]{2,1,0:T(8,128)(2,1)S(1)} %bitcast.92), channel_id=1, replica_groups=mesh['feat'=8,'rows'=16] {'rows'}, dimensions={0} | all-to-all | bytes 786432 | tf_op jit(solution)/shard_map/all_to_all | solution.py:101
  101.4 5.3 %collective-permute-done.4 = bf16[16,48,256]{2,1,0:T(8,128)(2,1)S(1)} collective-permute-done((bf16[16,48,256]{2,1,0:T(8,128)(2,1)S(1)}, bf16[16,48,256]{2,1,0:T(8,128)(2,1)S(1)}, u32[]{:S(2)}, u32[]{:S(2)}) %collective-permute-start.4) | collective-permute-done | bytes 393248 | tf_op jit(solution)/shard_map/ppermute | solution.py:119
  106.7 3.1 %collective-permute-start.5 = (bf16[16,48,256]{2,1,0:T(8,128)(2,1)S(1)}, bf16[16,48,256]{2,1,0:T(8,128)(2,1)S(1)}, u32[]{:S(2)}, u32[]{:S(2)}) collective-permute-start(bf16[16,48,256]{2,1,0:T(8,128)(2,1)S(1)} %collective-permute-done.4), channel_id=1, source_target_pairs={{0,112},{16,0},{32,16},{48,32},{64,48},{80,64},{96,80},{112,96},{1... | collective-permute-start | bytes 1179656 | tf_op jit(solution)/shard_map/ppermute | solution.py:119
  109.8 5.3 %collective-permute-done.5 = bf16[16,48,256]{2,1,0:T(8,128)(2,1)S(1)} collective-permute-done((bf16[16,48,256]{2,1,0:T(8,128)(2,1)S(1)}, bf16[16,48,256]{2,1,0:T(8,128)(2,1)S(1)}, u32[]{:S(2)}, u32[]{:S(2)}) %collective-permute-start.5) | collective-permute-done | bytes 393248 | tf_op jit(solution)/shard_map/ppermute | solution.py:119
  115.1 3.1 %collective-permute-start.6 = (bf16[16,48,256]{2,1,0:T(8,128)(2,1)S(1)}, bf16[16,48,256]{2,1,0:T(8,128)(2,1)S(1)}, u32[]{:S(2)}, u32[]{:S(2)}) collective-permute-start(bf16[16,48,256]{2,1,0:T(8,128)(2,1)S(1)} %collective-permute-done.5), channel_id=1, source_target_pairs={{0,112},{16,0},{32,16},{48,32},{64,48},{80,64},{96,80},{112,96},{1... | collective-permute-start | bytes 1179656 | tf_op jit(solution)/shard_map/ppermute | solution.py:119
  118.2 5.3 %collective-permute-done.6 = bf16[16,48,256]{2,1,0:T(8,128)(2,1)S(1)} collective-permute-done((bf16[16,48,256]{2,1,0:T(8,128)(2,1)S(1)}, bf16[16,48,256]{2,1,0:T(8,128)(2,1)S(1)}, u32[]{:S(2)}, u32[]{:S(2)}) %collective-permute-start.6) | collective-permute-done | bytes 393248 | tf_op jit(solution)/shard_map/ppermute | solution.py:119
  123.5 3.1 %collective-permute-start.7 = (bf16[16,48,256]{2,1,0:T(8,128)(2,1)S(1)}, bf16[16,48,256]{2,1,0:T(8,128)(2,1)S(1)}, u32[]{:S(2)}, u32[]{:S(2)}) collective-permute-start(bf16[16,48,256]{2,1,0:T(8,128)(2,1)S(1)} %collective-permute-done.6), channel_id=1, source_target_pairs={{0,112},{16,0},{32,16},{48,32},{64,48},{80,64},{96,80},{112,96},{1... | collective-permute-start | bytes 1179656 | tf_op jit(solution)/shard_map/ppermute | solution.py:119
  126.6 0.5 constant_dynamic-slice_fusion
  127.2 0.8 copy.43
  127.9 0.1 copy.44
  128.1 0.1 copy.45
  128.2 0.1 copy.46
  128.3 0.1 copy.47
  128.5 0.1 copy.48
  128.6 0.1 copy.49
  128.8 0.1 copy.50
  128.9 1.0 convolution_bitcast_fusion.8
  130.0 2.0 collective-permute-done.7
  131.9 3.1 %collective-permute-start.8 = (bf16[16,48,256]{2,1,0:T(8,128)(2,1)S(1)}, bf16[16,48,256]{2,1,0:T(8,128)(2,1)S(1)}, u32[]{:S(2)}, u32[]{:S(2)}) collective-permute-start(bf16[16,48,256]{2,1,0:T(8,128)(2,1)S(1)} %collective-permute-done.7), channel_id=1, source_target_pairs={{0,112},{16,0},{32,16},{48,32},{64,48},{80,64},{96,80},{112,96},{1... | collective-permute-start | bytes 1179656 | tf_op jit(solution)/shard_map/ppermute | solution.py:119
  135.0 0.2 fusion.15
  135.2 0.0 copy-done.9
  135.2 0.2 fusion.14
  135.5 4.9 %collective-permute-done.8 = bf16[16,48,256]{2,1,0:T(8,128)(2,1)S(1)} collective-permute-done((bf16[16,48,256]{2,1,0:T(8,128)(2,1)S(1)}, bf16[16,48,256]{2,1,0:T(8,128)(2,1)S(1)}, u32[]{:S(2)}, u32[]{:S(2)}) %collective-permute-start.8) | collective-permute-done | bytes 393248 | tf_op jit(solution)/shard_map/ppermute | solution.py:119
  140.3 3.1 %collective-permute-start.9 = (bf16[16,48,256]{2,1,0:T(8,128)(2,1)S(1)}, bf16[16,48,256]{2,1,0:T(8,128)(2,1)S(1)}, u32[]{:S(2)}, u32[]{:S(2)}) collective-permute-start(bf16[16,48,256]{2,1,0:T(8,128)(2,1)S(1)} %collective-permute-done.8), channel_id=1, source_target_pairs={{0,112},{16,0},{32,16},{48,32},{64,48},{80,64},{96,80},{112,96},{1... | collective-permute-start | bytes 1179656 | tf_op jit(solution)/shard_map/ppermute | solution.py:119
  143.4 0.2 fusion.13
  143.6 0.2 fusion.12
  143.9 4.9 %collective-permute-done.9 = bf16[16,48,256]{2,1,0:T(8,128)(2,1)S(1)} collective-permute-done((bf16[16,48,256]{2,1,0:T(8,128)(2,1)S(1)}, bf16[16,48,256]{2,1,0:T(8,128)(2,1)S(1)}, u32[]{:S(2)}, u32[]{:S(2)}) %collective-permute-start.9) | collective-permute-done | bytes 393248 | tf_op jit(solution)/shard_map/ppermute | solution.py:119
  148.7 3.1 %collective-permute-start.10 = (bf16[16,48,256]{2,1,0:T(8,128)(2,1)S(1)}, bf16[16,48,256]{2,1,0:T(8,128)(2,1)S(1)}, u32[]{:S(2)}, u32[]{:S(2)}) collective-permute-start(bf16[16,48,256]{2,1,0:T(8,128)(2,1)S(1)} %collective-permute-done.9), channel_id=1, source_target_pairs={{0,112},{16,0},{32,16},{48,32},{64,48},{80,64},{96,80},{112,96},{1... | collective-permute-start | bytes 1179656 | tf_op jit(solution)/shard_map/ppermute | solution.py:119
  151.9 0.2 fusion.11
  152.1 0.2 fusion.10
  152.3 4.9 %collective-permute-done.10 = bf16[16,48,256]{2,1,0:T(8,128)(2,1)S(1)} collective-permute-done((bf16[16,48,256]{2,1,0:T(8,128)(2,1)S(1)}, bf16[16,48,256]{2,1,0:T(8,128)(2,1)S(1)}, u32[]{:S(2)}, u32[]{:S(2)}) %collective-permute-start.10) | collective-permute-done | bytes 393248 | tf_op jit(solution)/shard_map/ppermute | solution.py:119
  157.2 0.2 fusion.9
  157.4 70.6 %psum.7 = f32[16,256]{1,0:T(8,128)} all-reduce(f32[16,256]{1,0:T(8,128)S(1)} %fusion.9), channel_id=1, replica_groups=mesh['feat'=8,'rows'=16] {'rows'}, use_global_device_ids=true, to_apply=%region_2.3 | all-reduce | flops 4096 | bytes 32768 | tf_op jit(solution)/shard_map/psum | solution.py:129
  (25 shorter events, 0.1 us)
Async XLA Ops:
  0.6 0.8 copy-start
  6.6 11.2 %copy-start.11 = (s32[6]{0:T(128)S(1)}, s32[6]{0:T(128)}, u32[]{:S(2)}) copy-start(s32[6]{0:T(128)} %param.16) | copy-start | bytes 76
  6.6 11.2 %copy-start.10 = (s32[6,8]{1,0:T(8,128)S(1)}, s32[6,8]{1,0:T(8,128)}, u32[]{:S(2)}) copy-start(s32[6,8]{1,0:T(8,128)} %param.15) | copy-start | bytes 580
  6.6 51.4 %all-to-all-start = ((bf16[128,48,256]{2,1,0:T(8,128)(2,1)}), bf16[128,48,256]{2,1,0:T(8,128)(2,1)S(1)}, u32[]{:S(2)}, u32[]{:S(2)}) async-start(bf16[128,48,256]{2,1,0:T(8,128)(2,1)} %copy.29), calls=%async_computation | async-start | bytes 6291456 | tf_op jit(solution)/shard_map/all_to_all | solution.py:60
  19.9 1.1 copy-start.2
  58.4 0.7 copy-start.5
  59.2 8.4 %collective-permute-start = (bf16[256,256]{1,0:T(8,128)(2,1)S(1)}, bf16[256,256]{1,0:T(8,128)(2,1)S(1)}, u32[]{:S(2)}, u32[]{:S(2)}) collective-permute-start(bf16[256,256]{1,0:T(8,128)(2,1)S(1)} %get-tuple-element.34), channel_id=1, source_target_pairs={{0,1},{1,2},{2,3},{3,4},{4,5},{5,6},{6,7},{7,8},{8,9},{9,10},{10,1... | collective-permute-start | bytes 393224 | tf_op jit(solution)/shard_map/ppermute | solution.py:16
  59.9 7.7 %collective-permute-start.1 = (bf16[256,256]{1,0:T(8,128)(2,1)S(1)}, bf16[256,256]{1,0:T(8,128)(2,1)S(1)}, u32[]{:S(2)}, u32[]{:S(2)}) collective-permute-start(bf16[256,256]{1,0:T(8,128)(2,1)S(1)} %get-tuple-element.35), channel_id=1, source_target_pairs={{1,0},{2,1},{3,2},{4,3},{5,4},{6,5},{7,6},{8,7},{9,8},{10,9},{11,1... | collective-permute-start | bytes 393224 | tf_op jit(solution)/shard_map/ppermute | solution.py:18
  68.6 2.6 %copy-start.3 = (bf16[6,8,128,128]{3,2,1,0:T(8,128)(2,1)S(1)}, bf16[6,8,128,128]{3,2,1,0:T(8,128)(2,1)}, u32[]{:S(2)}) copy-start(bf16[6,8,128,128]{3,2,1,0:T(8,128)(2,1)} %copy-done.2) | copy-start | bytes 4718596
  68.6 2.6 %copy-start.6 = (bf16[768,256]{1,0:T(8,128)(2,1)S(1)}, bf16[768,256]{1,0:T(8,128)(2,1)}, u32[]{:S(2)}) copy-start(bf16[768,256]{1,0:T(8,128)(2,1)} %copy-done.5) | copy-start | bytes 1179652
  68.6 2.6 %copy-start.12 = (f32[256]{0:T(256)S(1)}, f32[256]{0:T(256)}, u32[]{:S(2)}) copy-start(f32[256]{0:T(256)} %param.13) | copy-start | bytes 3076
  71.2 2.8 %copy-start.4 = (bf16[10,6,128,128]{3,0,2,1:T(8,128)(2,1)S(1)}, bf16[10,6,128,128]{3,0,2,1:T(8,128)(2,1)}, u32[]{:S(2)}) copy-start(bf16[10,6,128,128]{3,0,2,1:T(8,128)(2,1)} %convert_bitcast_fusion) | copy-start | bytes 5898244
  71.2 2.9 %copy-start.7 = (bf16[768,256]{1,0:T(8,128)(2,1)S(1)}, bf16[768,256]{1,0:T(8,128)(2,1)}, u32[]{:S(2)}) copy-start(bf16[768,256]{1,0:T(8,128)(2,1)} %param.17) | copy-start | bytes 1179652
  75.6 8.4 %collective-permute-start.2 = (bf16[2,128,256]{2,1,0:T(8,128)(2,1)S(1)}, bf16[2,128,256]{2,1,0:T(8,128)(2,1)S(1)}, u32[]{:S(2)}, u32[]{:S(2)}) collective-permute-start(bf16[2,128,256]{2,1,0:T(8,128)(2,1)S(1)} %get-tuple-element.33), channel_id=1, source_target_pairs={{15,0},{0,1},{1,2},{2,3},{3,4},{4,5},{5,6},{6,7},{7,8},{8,9},{9,10... | collective-permute-start | bytes 393224 | tf_op jit(solution)/shard_map/ppermute | solution.py:28
  77.1 49.6 %copy-start.1 = (bf16[16,128,48]{1,2,0:T(8,128)(2,1)S(1)}, bf16[16,128,48]{1,2,0:T(8,128)(2,1)}, u32[]{:S(2)}) copy-start(bf16[16,128,48]{1,2,0:T(8,128)(2,1)} %param.11) | copy-start | bytes 589828
  77.1 7.9 %collective-permute-start.3 = (bf16[2,128,256]{2,1,0:T(8,128)(2,1)S(1)}, bf16[2,128,256]{2,1,0:T(8,128)(2,1)S(1)}, u32[]{:S(2)}, u32[]{:S(2)}) collective-permute-start(bf16[2,128,256]{2,1,0:T(8,128)(2,1)S(1)} %get-tuple-element.32), channel_id=1, source_target_pairs={{1,0},{2,1},{3,2},{4,3},{5,4},{6,5},{7,6},{8,7},{9,8},{10,9},{11,1... | collective-permute-start | bytes 393224 | tf_op jit(solution)/shard_map/ppermute | solution.py:28
  101.4 5.3 %collective-permute-start.4 = (bf16[16,48,256]{2,1,0:T(8,128)(2,1)S(1)}, bf16[16,48,256]{2,1,0:T(8,128)(2,1)S(1)}, u32[]{:S(2)}, u32[]{:S(2)}) collective-permute-start(bf16[16,48,256]{2,1,0:T(8,128)(2,1)S(1)} %all_to_all.10), channel_id=1, source_target_pairs={{0,112},{16,0},{32,16},{48,32},{64,48},{80,64},{96,80},{112,96},{1... | collective-permute-start | bytes 1179656 | tf_op jit(solution)/shard_map/ppermute | solution.py:119
  106.7 8.4 %collective-permute-start.5 = (bf16[16,48,256]{2,1,0:T(8,128)(2,1)S(1)}, bf16[16,48,256]{2,1,0:T(8,128)(2,1)S(1)}, u32[]{:S(2)}, u32[]{:S(2)}) collective-permute-start(bf16[16,48,256]{2,1,0:T(8,128)(2,1)S(1)} %collective-permute-done.4), channel_id=1, source_target_pairs={{0,112},{16,0},{32,16},{48,32},{64,48},{80,64},{96,80},{112,96},{1... | collective-permute-start | bytes 1179656 | tf_op jit(solution)/shard_map/ppermute | solution.py:119
  115.1 11.5 %copy-start.8 = (bf16[16,48,256]{2,1,0:T(8,128)(2,1)}, bf16[16,48,256]{2,1,0:T(8,128)(2,1)S(1)}, u32[]{:S(2)}) copy-start(bf16[16,48,256]{2,1,0:T(8,128)(2,1)S(1)} %collective-permute-done.5) | copy-start | bytes 1179652
  115.1 8.4 %collective-permute-start.6 = (bf16[16,48,256]{2,1,0:T(8,128)(2,1)S(1)}, bf16[16,48,256]{2,1,0:T(8,128)(2,1)S(1)}, u32[]{:S(2)}, u32[]{:S(2)}) collective-permute-start(bf16[16,48,256]{2,1,0:T(8,128)(2,1)S(1)} %collective-permute-done.5), channel_id=1, source_target_pairs={{0,112},{16,0},{32,16},{48,32},{64,48},{80,64},{96,80},{112,96},{1... | collective-permute-start | bytes 1179656 | tf_op jit(solution)/shard_map/ppermute | solution.py:119
  123.5 8.4 %collective-permute-start.7 = (bf16[16,48,256]{2,1,0:T(8,128)(2,1)S(1)}, bf16[16,48,256]{2,1,0:T(8,128)(2,1)S(1)}, u32[]{:S(2)}, u32[]{:S(2)}) collective-permute-start(bf16[16,48,256]{2,1,0:T(8,128)(2,1)S(1)} %collective-permute-done.6), channel_id=1, source_target_pairs={{0,112},{16,0},{32,16},{48,32},{64,48},{80,64},{96,80},{112,96},{1... | collective-permute-start | bytes 1179656 | tf_op jit(solution)/shard_map/ppermute | solution.py:119
  128.1 7.2 %copy-start.9 = (bf16[16,48,256]{2,1,0:T(8,128)(2,1)S(1)}, bf16[16,48,256]{2,1,0:T(8,128)(2,1)}, u32[]{:S(2)}) copy-start(bf16[16,48,256]{2,1,0:T(8,128)(2,1)} %copy-done.8) | copy-start | bytes 1179652
  131.9 8.4 %collective-permute-start.8 = (bf16[16,48,256]{2,1,0:T(8,128)(2,1)S(1)}, bf16[16,48,256]{2,1,0:T(8,128)(2,1)S(1)}, u32[]{:S(2)}, u32[]{:S(2)}) collective-permute-start(bf16[16,48,256]{2,1,0:T(8,128)(2,1)S(1)} %collective-permute-done.7), channel_id=1, source_target_pairs={{0,112},{16,0},{32,16},{48,32},{64,48},{80,64},{96,80},{112,96},{1... | collective-permute-start | bytes 1179656 | tf_op jit(solution)/shard_map/ppermute | solution.py:119
  140.3 8.4 %collective-permute-start.9 = (bf16[16,48,256]{2,1,0:T(8,128)(2,1)S(1)}, bf16[16,48,256]{2,1,0:T(8,128)(2,1)S(1)}, u32[]{:S(2)}, u32[]{:S(2)}) collective-permute-start(bf16[16,48,256]{2,1,0:T(8,128)(2,1)S(1)} %collective-permute-done.8), channel_id=1, source_target_pairs={{0,112},{16,0},{32,16},{48,32},{64,48},{80,64},{96,80},{112,96},{1... | collective-permute-start | bytes 1179656 | tf_op jit(solution)/shard_map/ppermute | solution.py:119
  148.7 8.4 %collective-permute-start.10 = (bf16[16,48,256]{2,1,0:T(8,128)(2,1)S(1)}, bf16[16,48,256]{2,1,0:T(8,128)(2,1)S(1)}, u32[]{:S(2)}, u32[]{:S(2)}) collective-permute-start(bf16[16,48,256]{2,1,0:T(8,128)(2,1)S(1)} %collective-permute-done.9), channel_id=1, source_target_pairs={{0,112},{16,0},{32,16},{48,32},{64,48},{80,64},{96,80},{112,96},{1... | collective-permute-start | bytes 1179656 | tf_op jit(solution)/shard_map/ppermute | solution.py:119
